TPU v7x, 32 devices: a whole 2x2x4 slice. The times are simulated.
32 devices in a mesh: chain: 8 (over z, y), cand: 4 (over x, core).
Axes of the slice: x: 2, y: 2, z: 4, core: 2. Of those that a mesh axis runs over, the one named last changes fastest.
Arguments:
- archive_inputs: float32 [32, 1536], P(None, 'chain'), may hold values from -6 to 6
- candidate_inputs: float32 [32, 512], P(None, 'cand'), may hold values from -6 to 6
- lengthscales: float32 [32], replicated, may hold values from 3 to 10
- factor: float32 [1536, 1536], P('chain'), as said below
Outputs:
- whitened: float32 [1536, 512], P('chain', 'cand')
- corrected_cov: float32 [512, 512], P('chain', 'cand')
Inputs may be any that keep to these rules, and one draw needn't show every extreme that they name: factor is lower triangular (zeros above the diagonal); its diagonal lies between 0.2 * sqrt(1536) and 0.5 * sqrt(1536).
All inputs are finite; a program needn't handle non-finite values.
Results may differ from a plain program's by a relative error of at most 0.000076.
Values sent between devices are 32-bit elements; how exact they have to be, the bound alone decides.
A program may use at most 64 MiB of HBM per device.

v0:
```python
import jax
import jax.numpy as jnp
from jax import lax
from jax.sharding import PartitionSpec as P


def from_root(block, axis, source):
    block = jnp.where(lax.axis_index(axis) == source, block, jnp.zeros_like(block))
    return lax.psum(block, axis)


def matern(first_set, second_set):
    differ = first_set[:, :, None] - second_set[:, None, :]
    radius = jnp.sqrt(5.0 * jnp.sum(differ * differ, axis=0))
    return (1.0 + radius + radius * radius / 3.0) * jnp.exp(-radius)


def shards(archive_inputs, candidate_inputs, lengthscales, factor):
    height = factor.shape[0]
    column_count = candidate_inputs.shape[1]
    sections = lax.axis_size("chain")
    position = lax.axis_index("chain")
    scaling = 1.0 / lengthscales
    scaled_archive = archive_inputs * scaling[:, None]
    scaled_candidates = candidate_inputs * scaling[:, None]
    cross_tile = matern(scaled_archive, scaled_candidates)
    own_diagonal = lax.dynamic_slice_in_dim(factor, position * height, height, 1)
    inverse_block = jax.scipy.linalg.solve_triangular(
        own_diagonal, jnp.eye(height, dtype=jnp.float32), lower=True
    )

    def solve_own(residue):
        return jnp.dot(inverse_block, residue, precision=lax.Precision.HIGHEST)

    def skip_solve(residue):
        return jnp.zeros_like(residue)

    def advance(sender, state_pair):
        residue, stored = state_pair
        solved = lax.cond(position == sender, solve_own, skip_solve, residue)
        solved_panel = from_root(solved, "chain", sender)

        def apply_update(current):
            coupling = lax.dynamic_slice_in_dim(factor, sender * height, height, 1)
            return current - jnp.dot(coupling, solved_panel, precision=lax.Precision.HIGHEST)

        def keep_residue(current):
            return current

        residue = lax.cond(position > sender, apply_update, keep_residue, residue)
        stored = lax.dynamic_update_slice(
            stored, solved_panel[None], (sender, jnp.int32(0), jnp.int32(0))
        )
        return (residue, stored)

    initial = (cross_tile, jnp.zeros((sections, height, column_count), jnp.float32))
    residue, stored = lax.fori_loop(0, sections, advance, initial)
    own_panel = lax.dynamic_index_in_dim(stored, position, 0, keepdims=False)
    all_columns = column_count * lax.axis_size("cand")
    slab_width = all_columns // sections
    offset = position * slab_width
    whole_column = stored.reshape(sections * height, column_count)
    source = offset // column_count
    within = offset % column_count
    piece_whitened = lax.dynamic_slice_in_dim(whole_column, within, slab_width, 1)
    piece_inputs = lax.dynamic_slice_in_dim(candidate_inputs, within, slab_width, 1)
    remote_whitened, chosen = (
        from_root(piece_whitened, "cand", source),
        from_root(piece_inputs, "cand", source),
    )
    shared = jnp.dot(remote_whitened.T, whole_column, precision=lax.Precision.HIGHEST)
    prior_cov = matern(chosen * scaling[:, None], scaled_candidates)
    return (own_panel, prior_cov - shared)


def solution(mesh):
    return jax.shard_map(
        shards,
        mesh=mesh,
        in_specs=(P(None, "chain"), P(None, "cand"), P(), P("chain", None)),
        out_specs=(P("chain", "cand"), P("chain", "cand")),
        check_vma=False,
    )
```

profile of v0, /device:TPU:0, one launch (start us, length us, event | category | flops | bytes accessed | tf_op | source)
XLA Modules:
  0.0 684.6 jit_solution(12714835138368224703)
XLA Ops:
  8.1 1.1 dynamic-slice_select_fusion.1
  9.3 19.7 %custom-call.4 = f32[2,128,128]{1,2,0:T(8,128)S(1)} custom-call(f32[2,128,128]{2,1,0:T(8,128)S(1)} %pad_maximum_fusion.1), custom_call_target="InvertDiagBlocksLowerTriangular" | custom-call | tf_op jit(solution)/shard_map/jit(_solve_triangular)/triangular_solve | solution.py:28
  30.3 1.0 multiply_reduce_fusion
  31.4 605.9 %while.20 = (s32[]{:T(128)}, f32[192,128]{1,0:T(8,128)S(1)}, f32[8,192,128]{2,1,0:T(8,128)S(1)}, s32[]{:T(128)}, f32[192,192]{1,0:T(8,128)S(1)}, /*index=5*/f32[192,1536]{1,0:T(8,128)}, s32[]{:T(128)}, u32[]{:T(128)}, u32[]{:T(128)}) while((s32[]{:T(128)}, f32[192,128]{1,0:T(8,128)S(1)}, f32[8,192,128]{2,1,0:T(8,128)S(1)}, s32[]{:T(128)}, ...), condition=%wide.region_7.8_spmd, body=%wide.region_1.7_spmd.sunk | while | flops 113319944 | bytes 1818953 | solution.py:57
  32.5 75.8 %all-reduce.7.cloned.1.call-done = f32[192,128]{1,0:T(8,128)} async-done(((f32[192,128]{1,0:T(8,128)}), f32[192,128]{1,0:T(8,128)}) %all-reduce.7.cloned.1.call-update) | async-done | bytes 98320 | tf_op jit(solution)/shard_map/while/body/eval_jaxpr/psum | solution.py:9
  108.3 0.9 bitcast_dynamic-update-slice_fusion.2
  109.9 73.9 %all-reduce.7.cloned.1.call-done = f32[192,128]{1,0:T(8,128)} async-done(((f32[192,128]{1,0:T(8,128)}), f32[192,128]{1,0:T(8,128)}) %all-reduce.7.cloned.1.call-update) | async-done | bytes 98320 | tf_op jit(solution)/shard_map/while/body/eval_jaxpr/psum | solution.py:9
  183.8 0.9 bitcast_dynamic-update-slice_fusion.2
  185.5 73.9 %all-reduce.7.cloned.1.call-done = f32[192,128]{1,0:T(8,128)} async-done(((f32[192,128]{1,0:T(8,128)}), f32[192,128]{1,0:T(8,128)}) %all-reduce.7.cloned.1.call-update) | async-done | bytes 98320 | tf_op jit(solution)/shard_map/while/body/eval_jaxpr/psum | solution.py:9
  259.4 0.9 bitcast_dynamic-update-slice_fusion.2
  261.1 73.6 %all-reduce.7.cloned.1.call-done = f32[192,128]{1,0:T(8,128)} async-done(((f32[192,128]{1,0:T(8,128)}), f32[192,128]{1,0:T(8,128)}) %all-reduce.7.cloned.1.call-update) | async-done | bytes 98320 | tf_op jit(solution)/shard_map/while/body/eval_jaxpr/psum | solution.py:9
  334.7 0.9 bitcast_dynamic-update-slice_fusion.2
  336.4 73.6 %all-reduce.7.cloned.1.call-done = f32[192,128]{1,0:T(8,128)} async-done(((f32[192,128]{1,0:T(8,128)}), f32[192,128]{1,0:T(8,128)}) %all-reduce.7.cloned.1.call-update) | async-done | bytes 98320 | tf_op jit(solution)/shard_map/while/body/eval_jaxpr/psum | solution.py:9
  410.0 0.9 bitcast_dynamic-update-slice_fusion.2
  411.6 73.6 %all-reduce.7.cloned.1.call-done = f32[192,128]{1,0:T(8,128)} async-done(((f32[192,128]{1,0:T(8,128)}), f32[192,128]{1,0:T(8,128)}) %all-reduce.7.cloned.1.call-update) | async-done | bytes 98320 | tf_op jit(solution)/shard_map/while/body/eval_jaxpr/psum | solution.py:9
  485.2 0.9 bitcast_dynamic-update-slice_fusion.2
  486.9 73.9 %all-reduce.7.cloned.1.call-done = f32[192,128]{1,0:T(8,128)} async-done(((f32[192,128]{1,0:T(8,128)}), f32[192,128]{1,0:T(8,128)}) %all-reduce.7.cloned.1.call-update) | async-done | bytes 98320 | tf_op jit(solution)/shard_map/while/body/eval_jaxpr/psum | solution.py:9
  560.8 0.9 bitcast_dynamic-update-slice_fusion.2
  562.5 73.9 %all-reduce.7.cloned.1.call-done = f32[192,128]{1,0:T(8,128)} async-done(((f32[192,128]{1,0:T(8,128)}), f32[192,128]{1,0:T(8,128)}) %all-reduce.7.cloned.1.call-update) | async-done | bytes 98320 | tf_op jit(solution)/shard_map/while/body/eval_jaxpr/psum | solution.py:9
  636.4 0.9 bitcast_dynamic-update-slice_fusion.2
  637.3 1.2 dynamic-slice_select_fusion
  638.6 10.5 %psum.25 = f32[32,64]{1,0:T(8,128)S(1)} all-reduce(f32[32,64]{1,0:T(8,128)S(1)} %dynamic-slice_select_fusion.2), channel_id=1, replica_groups=mesh['chain'=8,'cand'=4] {'cand'}, use_global_device_ids=true, to_apply=%region_8.9 | all-reduce | flops 2048 | bytes 16384 | tf_op jit(solution)/shard_map/psum | solution.py:9
  650.2 23.8 %all-reduce.5.cloned.1.call-done = f32[1536,64]{1,0:T(8,128)} async-done(((f32[1536,64]{1,0:T(8,128)}), f32[1536,64]{1,0:T(8,128)}) %all-reduce.5.cloned.1.call-update) | async-done | bytes 393232 | tf_op jit(solution)/shard_map/psum | solution.py:9
  674.0 3.2 convolution_subtract_fusion.2
  (76 shorter events, 9.2 us)
Async XLA Ops:
  8.1 22.0 %copy-start.2 = (f32[32]{0:T(128)S(1)}, f32[32]{0:T(128)}, u32[]{:S(2)}) copy-start(f32[32]{0:T(128)} %param.12) | copy-start | bytes 388
  8.1 22.0 %copy-start = (f32[32,128]{1,0:T(8,128)S(1)}, f32[32,128]{1,0:T(8,128)}, u32[]{:S(2)}) copy-start(f32[32,128]{1,0:T(8,128)} %param.11) | copy-start | bytes 49156
  8.1 22.1 %copy-start.1 = (f32[32,192]{1,0:T(8,128)S(1)}, f32[32,192]{1,0:T(8,128)}, u32[]{:S(2)}) copy-start(f32[32,192]{1,0:T(8,128)} %param.10) | copy-start | bytes 73732
  31.4 76.9 %all-reduce.7.cloned.1.call-start = ((), (), s32[]{:S(2)}) async-start(), calls=%async_computation.1 | async-start | bytes 196608 | tf_op jit(solution)/shard_map/while/body/eval_jaxpr/psum | solution.py:9
  109.2 74.7 %all-reduce.7.cloned.1.call-start = ((), (), s32[]{:S(2)}) async-start(), calls=%async_computation.1 | async-start | bytes 196608 | tf_op jit(solution)/shard_map/while/body/eval_jaxpr/psum | solution.py:9
  184.7 74.7 %all-reduce.7.cloned.1.call-start = ((), (), s32[]{:S(2)}) async-start(), calls=%async_computation.1 | async-start | bytes 196608 | tf_op jit(solution)/shard_map/while/body/eval_jaxpr/psum | solution.py:9
  260.3 74.4 %all-reduce.7.cloned.1.call-start = ((), (), s32[]{:S(2)}) async-start(), calls=%async_computation.1 | async-start | bytes 196608 | tf_op jit(solution)/shard_map/while/body/eval_jaxpr/psum | solution.py:9
  335.6 74.4 %all-reduce.7.cloned.1.call-start = ((), (), s32[]{:S(2)}) async-start(), calls=%async_computation.1 | async-start | bytes 196608 | tf_op jit(solution)/shard_map/while/body/eval_jaxpr/psum | solution.py:9
  410.9 74.4 %all-reduce.7.cloned.1.call-start = ((), (), s32[]{:S(2)}) async-start(), calls=%async_computation.1 | async-start | bytes 196608 | tf_op jit(solution)/shard_map/while/body/eval_jaxpr/psum | solution.py:9
  486.1 74.7 %all-reduce.7.cloned.1.call-start = ((), (), s32[]{:S(2)}) async-start(), calls=%async_computation.1 | async-start | bytes 196608 | tf_op jit(solution)/shard_map/while/body/eval_jaxpr/psum | solution.py:9
  561.7 74.7 %all-reduce.7.cloned.1.call-start = ((), (), s32[]{:S(2)}) async-start(), calls=%async_computation.1 | async-start | bytes 196608 | tf_op jit(solution)/shard_map/while/body/eval_jaxpr/psum | solution.py:9
  637.3 36.7 %all-reduce.5.cloned.1.call-start = ((), (), s32[]{:S(2)}) async-start(), calls=%async_computation | async-start | bytes 1572864 | tf_op jit(solution)/shard_map/psum | solution.py:9
Sparse Core Ops, SparseCore 0:
  36.2 72.0 all-reduce.6
  113.9 69.8 all-reduce.6
  189.5 69.8 all-reduce.6
  264.8 69.8 all-reduce.6
  340.1 69.8 all-reduce.6
  415.3 69.8 all-reduce.6
  490.9 69.8 all-reduce.6
  566.5 69.8 all-reduce.6
Sparse Core Ops, SparseCore 1:
  640.1 33.9 all-reduce.4
where the time goes:
time: 685 us
  waiting for transfers between devices  616 us (90%)
  other arithmetic  29 us (4%)
  between operations  15.7 us (2%)
  blocking collectives  10.5 us (2%)
  local copies, waits for them, and re-layouts  8.04 us (1%)
    psum x9, waiting for transfers between devices, from_root(): return lax.psum(block, axis)  616 us
    another operation x7, other arithmetic, shards(): jax.scipy.linalg.solve_triangular(own_diagonal, jnp.eye(height, dtype=jnp...  20.9 us
  transfers between devices with their start and end apart: 9, of which 9 were waited for; matrix products, arithmetic and copies ran while one was open for 0% of the time, Pallas kernels for 0%

commit v1 on v0

v1 whole, which is shorter than its diff:
```python
import functools
import jax
import jax.numpy as jnp
from jax import lax
from jax.experimental import pallas as pl
from jax.experimental.pallas import tpu as pltpu
from jax.sharding import PartitionSpec as P

MESH = pl.DeviceIdType.MESH
F32 = jnp.float32
BASE = 16


def split(value):
    high = value.astype(jnp.bfloat16)
    return high, (value - high.astype(F32)).astype(jnp.bfloat16)


def product(first, second, transposed=False):
    dims = (((1,), (1 if transposed else 0,)), ((), ()))
    dot = functools.partial(lax.dot_general, dimension_numbers=dims, preferred_element_type=F32)
    return dot(first[0], second[0]) + (dot(first[0], second[1]) + dot(first[1], second[0]))


def matern(rows, columns):
    total = None
    for d in range(columns.shape[0]):
        differ = rows[:, d:d + 1] - columns[d:d + 1, :]
        total = differ * differ if total is None else total + differ * differ
    radius = jnp.sqrt(5.0 * total)
    return (1.0 + radius + radius * radius / 3.0) * jnp.exp(-radius)


def base_inverse(block):
    size = block.shape[0]
    count = size // BASE
    row = lax.broadcasted_iota(jnp.int32, (size, size), 0)
    column = lax.broadcasted_iota(jnp.int32, (size, size), 1)
    same = (row // BASE) == (column // BASE)
    kept = jnp.where(same, block, 0.0)
    packed = functools.reduce(jnp.add, [kept[b * BASE:(b + 1) * BASE] for b in range(count)])
    lane = lax.broadcasted_iota(jnp.int32, (BASE, size), 1) % BASE
    sub = lax.broadcasted_iota(jnp.int32, (BASE, size), 0)
    picked = jnp.concatenate([jnp.where(lane == k, packed, 0.0) for k in range(BASE)], axis=0)
    group = same.astype(F32).astype(jnp.bfloat16)
    spread = None
    rest = picked
    for _ in range(3):
        part = rest.astype(jnp.bfloat16)
        rest = rest - part.astype(F32)
        term = jnp.dot(part, group, preferred_element_type=F32)
        spread = term if spread is None else spread + term
    state = jnp.where(sub == lane, 1.0, 0.0).astype(F32)
    for k in range(BASE):
        coupling = spread[k * BASE:(k + 1) * BASE]
        solved = state[k:k + 1] * (1.0 / coupling[k:k + 1])
        state = jnp.where(sub == k, solved, jnp.where(sub > k, state - coupling * solved, state))
    return jnp.where(same, jnp.concatenate([state] * count, axis=0), 0.0)


def grow_inverse(block, inverse):
    size = block.shape[0]
    row = lax.broadcasted_iota(jnp.int32, (size, size), 0)
    column = lax.broadcasted_iota(jnp.int32, (size, size), 1)
    width = BASE
    while width < size:
        below = ((row // width) == (column // width) + 1) & ((row // (2 * width)) == (column // (2 * width)))
        parts = split(inverse)
        middle = product(parts, split(jnp.where(below, block, 0.0)))
        inverse = inverse - product(split(middle), parts)
        width *= 2
    return inverse


def kernel(sections, cands, archive, candidates, lengths, factor, whitened, covariance,
           both_archive, chosen, points, unit, joined_high, joined_low, panels, peers, columns,
           turned, sums, pieces,
           in_send, in_recv, ch_send, ch_recv, y_send, y_recv, s_send, s_recv,
           pan_send, pan_recv, out_send, out_recv, pass_send, peer_recv, sum_send, sum_recv):
    me = lax.axis_index("chain")
    c = lax.axis_index("cand")
    z, y = me // 2, me % 2
    steps = sections // 2
    core = c % 2
    height = factor.shape[0]
    pair = 2 * height
    width = candidates.shape[1]
    half = width // 2
    ratio = (2 * cands) // sections
    slab = half * ratio
    strip = height // 2
    partner = 2 * z + (1 - y)
    sibling = c + 1 - 2 * core

    def remote(source, target, send, recv, where):
        return pltpu.make_async_remote_copy(
            src_ref=source, dst_ref=target, send_sem=send, recv_sem=recv, device_id=where, device_id_type=MESH)

    barrier = pltpu.get_barrier_semaphore()
    for d in range(1, sections):
        pl.semaphore_signal(barrier, inc=1, device_id=(lax.rem(me + d, sections), c), device_id_type=MESH)
    for d in range(1, cands):
        pl.semaphore_signal(barrier, inc=1, device_id=(me, lax.rem(c + d, cands)), device_id_type=MESH)

    strip_of_pair = factor[:, pl.ds(pl.multiple_of(z * pair, 128), pair)]
    block = jnp.where(y == 0, strip_of_pair[:, :height], strip_of_pair[:, height:])
    small = base_inverse(block)
    scaling = 1.0 / lengths[...]
    both_archive[y] = archive[...]
    owner_cand = (me * slab) // width

    pl.semaphore_wait(barrier, sections + cands - 2)

    send_in = remote(archive, both_archive.at[y], in_send, in_recv, (partner, c))
    send_in.start()

    def chosen_copy(d):
        return remote(candidates, chosen, ch_send.at[d - 1], ch_recv, (me, lax.rem(c + d, cands)))

    @pl.when(c == owner_cand)
    def _():
        for d in range(1, cands):
            chosen_copy(d).start()
        chosen[...] = candidates[...]

    inverse = grow_inverse(block, small)
    inverse_parts = split(inverse)
    zeros = jnp.zeros((height, height), F32)
    lane = lax.broadcasted_iota(jnp.int32, (height, pair), 1)
    near = product(inverse_parts, split(strip_of_pair))
    unit[0, y] = jnp.where(
        y == 0, jnp.concatenate([inverse, zeros], axis=1),
        jnp.where(lane < height, near, jnp.concatenate([zeros, inverse], axis=1)))

    mine = pl.ds(pl.multiple_of(core * strip, 8), strip)
    others = pl.ds(pl.multiple_of((1 - core) * strip, 8), strip)

    def across(e):
        area = unit.at[e, y, mine]
        return remote(area, area, y_send.at[e], y_recv.at[e], (partner, c))

    def across_recv(e):
        area = unit.at[e, 1 - y, mine]
        return remote(area, area, y_send.at[e], y_recv.at[e], (partner, c))

    def beside(e):
        area = unit.at[e, 1 - y, mine]
        return remote(area, area, s_send.at[e], s_recv.at[e], (me, sibling))

    def beside_recv(e):
        area = unit.at[e, 1 - y, others]
        return remote(area, area, s_send.at[e], s_recv.at[e], (me, sibling))

    across(0).start()
    for j in range(steps - 1):
        @pl.when(z > j)
        def _(j=j):
            unit[j + 1, y] = product(inverse_parts, split(factor[:, j * pair:(j + 1) * pair]))
            across(j + 1).start()

    points[...] = jnp.transpose(candidates[...] * scaling)
    own_points = points[pl.ds(pl.multiple_of(y * half, 8), half), :]
    send_in.wait_send()
    remote(archive, both_archive.at[1 - y], in_send, in_recv, (partner, c)).wait_recv()
    both = jnp.concatenate([both_archive[0], both_archive[1]], axis=1) * scaling
    cross = matern(own_points, both)

    across_recv(0).wait_recv()
    beside(0).start()
    for j in range(steps - 1):
        @pl.when(z > j)
        def _(j=j):
            across_recv(j + 1).wait_recv()
            beside(j + 1).start()
    beside_recv(0).wait_recv()
    upper = unit[0, 0]
    lower = unit[0, 1]
    full = jnp.concatenate(
        [jnp.where(lane < height, upper, 0.0), jnp.where(lane < height, 0.0, lower)], axis=0)
    columns[y] = product(split(cross), split(full), transposed=True)
    high, low = split(jnp.concatenate(
        [jnp.zeros((height, pair), F32), jnp.where(lane < height, lower, 0.0)], axis=0))
    joined_high[0] = high
    joined_low[0] = low

    def onward(j):
        return remote(panels.at[j], panels.at[j], pan_send.at[j], pan_recv.at[j],
                      (lax.rem(me + 2, sections), c))

    for j in range(steps - 1):
        @pl.when(z > j)
        def _(j=j):
            beside_recv(j + 1).wait_recv()
            high, low = split(unit[j + 1].reshape(pair, pair))
            joined_high[j + 1] = high
            joined_low[j + 1] = low
            onward(j).wait_recv()
            if j < steps - 2:
                @pl.when(z < steps - 1)
                def _():
                    onward(j).start()
            columns[y] = columns[y] - product(
                split(panels[j]), (joined_high[j + 1], joined_low[j + 1]), transposed=True)

    reduced = columns[y]
    solved = reduced - product(split(reduced), (joined_high[0], joined_low[0]), transposed=True)
    columns[y] = solved

    def launch(j):
        return remote(columns.at[y], panels.at[j], out_send.at[0], pan_recv.at[j], (lax.rem(me + 2, sections), c))

    for j in range(steps - 1):
        @pl.when(z == j)
        def _(j=j):
            launch(j).start()

    def to_peer(d):
        return remote(columns.at[y], peers.at[c], out_send.at[1 + d], peer_recv.at[c], (me, lax.rem(c + 2 * d, cands)))

    def from_peer(q):
        return remote(columns.at[y], peers.at[q], out_send.at[1], peer_recv.at[q], (me, sibling))

    def pass_on(d):
        q = lax.rem(c + 2 * d, cands)
        return remote(peers.at[q], peers.at[q], pass_send.at[d], peer_recv.at[q], (me, sibling))

    half_count = cands // 2
    for d in range(1, half_count):
        to_peer(d).start()
    to_sibling = remote(columns.at[y], peers.at[c], out_send.at[1], peer_recv.at[c], (me, sibling))
    to_sibling.start()
    to_partner = remote(columns.at[y], columns.at[y], out_send.at[1 + half_count], out_recv, (partner, c))
    to_partner.start()
    peers[c] = solved

    @pl.when(c != owner_cand)
    def _():
        remote(candidates, chosen, ch_send.at[0], ch_recv, (me, sibling)).wait_recv()

    points[...] = jnp.transpose(chosen[...] * scaling)
    within = pl.multiple_of((me * slab) % width, 8)
    prior = matern(points[pl.ds(within, slab), :], candidates[...] * scaling)
    covariance[...] = prior

    for d in range(1, half_count):
        q = lax.rem(c + 2 * d, cands)
        from_peer(q).wait_recv()
        pass_on(d).start()
    remote(columns.at[y], columns.at[1 - y], out_send.at[1], out_recv, (partner, c)).wait_recv()
    own_columns = columns[...].reshape(width, pair)
    for d in range(half_count):
        from_peer(lax.rem(sibling + 2 * d, cands)).wait_recv()

    gram = product(split(peers[...].reshape(cands * half, pair)), split(own_columns), transposed=True)
    pieces[...] = gram.reshape(cands, half, width)

    def piece_copy(q):
        group = 2 * q + y
        return remote(pieces.at[q], sums.at[z, group % ratio], sum_send.at[q],
                      sum_recv.at[z, group % ratio], (group // ratio, c))

    for q in range(cands):
        group = 2 * q + y

        @pl.when(group // ratio != me)
        def _(q=q):
            piece_copy(q).start()

        @pl.when(group // ratio == me)
        def _(q=q, group=group):
            sums[z, group % ratio] = pieces[q]

    turned[...] = jnp.transpose(own_columns)
    whitened[...] = turned[pl.ds(pl.multiple_of(y * height, 8), height), :]

    for k in range(ratio):
        for step in range(steps):
            sender = 2 * step + lax.rem(ratio * me + k, 2)

            @pl.when(sender != me)
            def _(k=k, step=step):
                remote(pieces.at[0], sums.at[step, k], sum_send.at[0], sum_recv.at[step, k], (partner, c)).wait_recv()
        total = functools.reduce(jnp.add, [sums[step, k] for step in range(steps)])
        covariance[k * half:(k + 1) * half] = covariance[k * half:(k + 1) * half] - total

    @pl.when(c == owner_cand)
    def _():
        for d in range(1, cands):
            chosen_copy(d).wait_send()
    across(0).wait_send()
    beside(0).wait_send()
    for j in range(steps - 1):
        @pl.when(z > j)
        def _(j=j):
            across(j + 1).wait_send()
            beside(j + 1).wait_send()
            if j < steps - 2:
                @pl.when(z < steps - 1)
                def _():
                    onward(j).wait_send()

        @pl.when(z == j)
        def _(j=j):
            launch(j).wait_send()
    for d in range(1, half_count):
        to_peer(d).wait_send()
        pass_on(d).wait_send()
    to_sibling.wait_send()
    to_partner.wait_send()
    for q in range(cands):
        @pl.when((2 * q + y) // ratio != me)
        def _(q=q):
            piece_copy(q).wait_send()


def shards(sections, cands, archive, candidates, lengths, factor):
    dims, height = archive.shape
    width = candidates.shape[1]
    pair, half, steps = 2 * height, width // 2, sections // 2
    ratio = (2 * cands) // sections
    vmem = pl.BlockSpec(memory_space=pltpu.VMEM)
    dma = pltpu.SemaphoreType.DMA
    return pl.pallas_call(
        functools.partial(kernel, sections, cands),
        out_shape=(jax.ShapeDtypeStruct((height, width), F32), jax.ShapeDtypeStruct((half * ratio, width), F32)),
        in_specs=[vmem] * 4,
        out_specs=(vmem, vmem),
        scratch_shapes=[
            pltpu.VMEM((2, dims, height), F32),
            pltpu.VMEM((dims, width), F32),
            pltpu.VMEM((width, dims), F32),
            pltpu.VMEM((steps, 2, height, pair), F32),
            pltpu.VMEM((steps, pair, pair), jnp.bfloat16),
            pltpu.VMEM((steps, pair, pair), jnp.bfloat16),
            pltpu.VMEM((steps - 1, half, pair), F32),
            pltpu.VMEM((cands, half, pair), F32),
            pltpu.VMEM((2, half, pair), F32),
            pltpu.VMEM((pair, width), F32),
            pltpu.VMEM((steps, ratio, half, width), F32),
            pltpu.VMEM((cands, half, width), F32),
            dma, dma,
            dma((cands - 1,)), dma,
            dma((steps,)), dma((steps,)), dma((steps,)), dma((steps,)),
            dma((steps - 1,)), dma((steps - 1,)),
            dma((2 + cands // 2,)), dma,
            dma((cands // 2,)), dma((cands,)),
            dma((cands,)), dma((steps, ratio)),
        ],
        compiler_params=pltpu.CompilerParams(
            collective_id=0, has_side_effects=True, vmem_limit_bytes=40 * 1024 * 1024),
    )(archive, candidates, lengths.reshape(dims, 1), factor)


def solution(mesh):
    return jax.shard_map(
        functools.partial(shards, mesh.shape["chain"], mesh.shape["cand"]),
        mesh=mesh,
        in_specs=(P(None, "chain"), P(None, "cand"), P(), P("chain", None)),
        out_specs=(P("chain", "cand"), P("chain", "cand")),
        check_vma=False,
    )
```

time: 685 us -> 47.6 us (0.07)
  waiting for transfers between devices: 616 us -> 0 us
  Pallas kernels: 0 us -> 41.8 us
  other arithmetic: 29 us -> 0 us
  between operations: 15.7 us -> 0.64 us
  blocking collectives: 10.5 us -> 0 us
    psum x9 -> x0, waiting for transfers between devices: 616 us -> none  [from_root(): return lax.psum(block, axis)]
    pallas_call x0 -> x1, Pallas kernels: none -> 41.8 us  [shards(): pl.pallas_call(functools.partial(kernel, sections, cands), out_shape=(jax...]
    another operation x7 -> x0, other arithmetic: 20.9 us -> none  [shards(): jax.scipy.linalg.solve_triangular(own_diagonal, jnp.eye(height, dtype=jnp...]
    psum x1 -> x0, blocking collectives: 10.5 us -> none  [from_root(): return lax.psum(block, axis)]
    dynamic_update_slice x8 -> x0, local copies, waits for them, and re-layouts: 7.2 us -> none  [advance(): lax.dynamic_update_slice(stored, solved_panel[None], (sender, jnp.int32(0...]
  transfers between devices with their start and end apart: 9 -> 0, of which waited for: 9 -> 0; matrix products, arithmetic and copies ran while one was open for 0% -> 0% of each run, Pallas kernels for 0% -> 0%
where the time goes in v1:
time: 47.6 us; the launch traced here: 47.2 us
  Pallas kernels  41.8 us (88%)
  local copies, waits for them, and re-layouts  4.74 us (10%)
  between operations  0.64 us (1%)
    pallas_call x1, Pallas kernels, shards(): pl.pallas_call(functools.partial(kernel, sections, cands), out_shape=(jax...  41.8 us
    unnamed x8, local copies, waits for them, and re-layouts  4 us

profile of v1, /device:TPU:0, one launch (start us, length us, event | category | flops | bytes accessed | tf_op | source)
XLA Modules:
  0.0 47.2 jit_solution(15624628152921803927)
XLA Ops:
  0.6 0.7 %copy.6.lengths = f32[32,1]{1,0:T(8,128)S(1)} copy(f32[32,1]{0,1:T(1,128)} %bitcast.1) | data formatting | bytes 256 | tf_op jit(solution)/shard_map/reshape | solution.py:351
  1.4 0.0 copy-start
  1.4 1.3 %copy-done = f32[192,1536]{1,0:T(8,128)S(1)} copy-done((f32[192,1536]{1,0:T(8,128)S(1)}, f32[192,1536]{1,0:T(8,128)}, u32[]{:S(2)}) %copy-start) | copy-done | bytes 1179672
  2.6 0.0 copy-start.1
  2.6 0.8 %copy-done.1 = f32[32,192]{1,0:T(8,128)S(1)} copy-done((f32[32,192]{1,0:T(8,128)S(1)}, f32[32,192]{1,0:T(8,128)}, u32[]{:S(2)}) %copy-start.1) | copy-done | bytes 24600
  3.4 0.0 copy-start.2
  3.4 0.7 %copy-done.2 = f32[32,128]{1,0:T(8,128)S(1)} copy-done((f32[32,128]{1,0:T(8,128)S(1)}, f32[32,128]{1,0:T(8,128)}, u32[]{:S(2)}) %copy-start.2) | copy-done | bytes 16408
  4.1 41.8 %shard_map.59 = (f32[192,128]{1,0:T(8,128)S(1)}, f32[64,128]{1,0:T(8,128)S(1)}) custom-call(f32[32,192]{1,0:T(8,128)S(1)} %copy-done.1, f32[32,128]{1,0:T(8,128)S(1)} %copy-done.2, f32[32,1]{1,0:T(8,128)S(1)} %copy.6.lengths, f32[192,1536]{1,0:T(8,128)S(1)} %copy-done), custom_call_target="tpu_custom_call" | custom-call | tf_op jit(solution)/shard_map/pallas_call | solution.py:323
  46.0 0.6 %copy.9 = f32[192,128]{1,0:T(8,128)} copy(f32[192,128]{1,0:T(8,128)S(1)} %get-tuple-element.4) | data formatting | bytes 196608
  46.6 0.6 %copy.10 = f32[64,128]{1,0:T(8,128)} copy(f32[64,128]{1,0:T(8,128)S(1)} %get-tuple-element.5) | data formatting | bytes 65536
Async XLA Ops:
  1.4 1.3 %copy-start = (f32[192,1536]{1,0:T(8,128)S(1)}, f32[192,1536]{1,0:T(8,128)}, u32[]{:S(2)}) copy-start(f32[192,1536]{1,0:T(8,128)} %factor.1) | copy-start | bytes 3538948
  2.6 0.8 %copy-start.1 = (f32[32,192]{1,0:T(8,128)S(1)}, f32[32,192]{1,0:T(8,128)}, u32[]{:S(2)}) copy-start(f32[32,192]{1,0:T(8,128)} %archive.1) | copy-start | bytes 73732
  3.4 0.7 %copy-start.2 = (f32[32,128]{1,0:T(8,128)S(1)}, f32[32,128]{1,0:T(8,128)}, u32[]{:S(2)}) copy-start(f32[32,128]{1,0:T(8,128)} %candidates.1) | copy-start | bytes 49156

commit v2 on v1

v2 whole, which is shorter than its diff:
```python
import functools
import jax
import jax.numpy as jnp
from jax import lax
from jax.experimental import pallas as pl
from jax.experimental.pallas import tpu as pltpu
from jax.sharding import PartitionSpec as P

MESH = pl.DeviceIdType.MESH
F32 = jnp.float32
BASE = 16


def split(value):
    high = value.astype(jnp.bfloat16)
    return high, (value - high.astype(F32)).astype(jnp.bfloat16)


def product(first, second, transposed=False):
    dims = (((1,), (1 if transposed else 0,)), ((), ()))
    dot = functools.partial(lax.dot_general, dimension_numbers=dims, preferred_element_type=F32)
    return dot(first[0], second[0]) + (dot(first[0], second[1]) + dot(first[1], second[0]))


def matern(rows, columns):
    total = None
    for d in range(columns.shape[0]):
        differ = rows[:, d:d + 1] - columns[d:d + 1, :]
        total = differ * differ if total is None else total + differ * differ
    radius = jnp.sqrt(5.0 * total)
    return (1.0 + radius + radius * radius / 3.0) * jnp.exp(-radius)


def base_inverse(block):
    size = block.shape[0]
    count = size // BASE
    row = lax.broadcasted_iota(jnp.int32, (size, size), 0)
    column = lax.broadcasted_iota(jnp.int32, (size, size), 1)
    same = (row // BASE) == (column // BASE)
    kept = jnp.where(same, block, 0.0)
    packed = functools.reduce(jnp.add, [kept[b * BASE:(b + 1) * BASE] for b in range(count)])
    lane = lax.broadcasted_iota(jnp.int32, (BASE, size), 1) % BASE
    sub = lax.broadcasted_iota(jnp.int32, (BASE, size), 0)
    picked = jnp.concatenate([jnp.where(lane == k, packed, 0.0) for k in range(BASE)], axis=0)
    group = same.astype(F32).astype(jnp.bfloat16)
    spread = None
    rest = picked
    for _ in range(3):
        part = rest.astype(jnp.bfloat16)
        rest = rest - part.astype(F32)
        term = jnp.dot(part, group, preferred_element_type=F32)
        spread = term if spread is None else spread + term
    state = jnp.where(sub == lane, 1.0, 0.0).astype(F32)
    for k in range(BASE):
        coupling = spread[k * BASE:(k + 1) * BASE]
        solved = state[k:k + 1] * (1.0 / coupling[k:k + 1])
        state = jnp.where(sub == k, solved, jnp.where(sub > k, state - coupling * solved, state))
    return jnp.where(same, jnp.concatenate([state] * count, axis=0), 0.0)


def grow_inverse(block, inverse):
    size = block.shape[0]
    row = lax.broadcasted_iota(jnp.int32, (size, size), 0)
    column = lax.broadcasted_iota(jnp.int32, (size, size), 1)
    width = BASE
    while width < size:
        above = ((row // width) + 1 == (column // width)) & ((row // (2 * width)) == (column // (2 * width)))
        parts = split(inverse)
        middle = product(parts, split(jnp.where(above, block, 0.0)))
        inverse = inverse - product(split(middle), parts)
        width *= 2
    return inverse


def kernel(sections, cands, archive, candidates, lengths, factor, whitened, covariance,
           both_archive, near, far, own_candidates, own_lengths, chosen, points, inverses,
           high_weights, low_weights, panels, peers, columns, turned, sums, pieces,
           load, far_load, in_send, in_recv, ch_send, ch_recv, y_send, y_recv, s_send, s_recv,
           pan_send, pan_recv, out_send, out_recv, pass_send, peer_recv, sum_send, sum_recv):
    me = lax.axis_index("chain")
    c = lax.axis_index("cand")
    z, y = me // 2, me % 2
    steps = sections // 2
    core = c % 2
    height = factor.shape[0]
    pair = 2 * height
    cover = -(-height // 128) * 128
    width = candidates.shape[1]
    half = width // 2
    ratio = (2 * cands) // sections
    slab = half * ratio
    strip = height // 2
    partner = 2 * z + (1 - y)
    sibling = c + 1 - 2 * core
    mine = pl.ds(pl.multiple_of(core * strip, 8), strip)
    others = pl.ds(pl.multiple_of((1 - core) * strip, 8), strip)
    diagonal = pl.multiple_of(z * pair, 128)

    def remote(source, target, send, recv, where):
        return pltpu.make_async_remote_copy(
            src_ref=source, dst_ref=target, send_sem=send, recv_sem=recv, device_id=where, device_id_type=MESH)

    def far_copy(j):
        return pltpu.make_async_copy(factor.at[:, j * pair:(j + 1) * pair], far.at[j, y], far_load.at[j])

    near_copy = pltpu.make_async_copy(factor.at[:, pl.ds(diagonal, pair)], near.at[y], load.at[0])
    lengths_copy = pltpu.make_async_copy(lengths, own_lengths, load.at[1])
    candidates_copy = pltpu.make_async_copy(candidates, own_candidates, load.at[2])
    archive_copy = pltpu.make_async_copy(archive, both_archive.at[y], load.at[3])
    near_copy.start()
    lengths_copy.start()
    candidates_copy.start()
    archive_copy.start()

    barrier = pltpu.get_barrier_semaphore()
    for d in range(1, sections):
        pl.semaphore_signal(barrier, inc=1, device_id=(lax.rem(me + d, sections), c), device_id_type=MESH)
    for d in range(1, cands):
        pl.semaphore_signal(barrier, inc=1, device_id=(me, lax.rem(c + d, cands)), device_id_type=MESH)
    for j in range(steps - 1):
        @pl.when(z > j)
        def _(j=j):
            far_copy(j).start()

    near_copy.wait()
    strip_of_pair = near[y]
    block = jnp.where(y == 0, strip_of_pair[:, :height], strip_of_pair[:, height:])
    small = jnp.transpose(base_inverse(block))
    block = jnp.transpose(block)
    lengths_copy.wait()
    candidates_copy.wait()
    archive_copy.wait()
    scale_row = 1.0 / own_lengths[...]
    scaling = jnp.transpose(jnp.broadcast_to(scale_row, (8, scale_row.shape[1])))[:, :1]
    owner_cand = (me * slab) // width

    pl.semaphore_wait(barrier, sections + cands - 2)

    send_in = remote(archive, both_archive.at[y], in_send, in_recv, (partner, c))
    send_in.start()

    def area(e, who, rows):
        if e == 0:
            return inverses.at[who, rows]
        if e == 1:
            return near.at[1, rows, pl.ds(0, cover)]
        return far.at[e - 2, who, rows]

    def across(e):
        if e == 0:
            source = inverses.at[y, mine]
        elif e == 1:
            source = factor.at[mine, pl.ds(diagonal, cover)]
        else:
            source = factor.at[mine, pl.ds((e - 2) * pair, pair)]
        return remote(source, area(e, y, mine), y_send.at[e], y_recv.at[e], (partner, c))

    def across_recv(e):
        return remote(area(e, 1 - y, mine), area(e, 1 - y, mine), y_send.at[e], y_recv.at[e], (partner, c))

    def beside(e):
        return remote(area(e, 1 - y, mine), area(e, 1 - y, mine), s_send.at[e], s_recv.at[e], (me, sibling))

    def beside_recv(e):
        return remote(area(e, 1 - y, others), area(e, 1 - y, others), s_send.at[e], s_recv.at[e], (me, sibling))

    @pl.when(y == 1)
    def _():
        across(1).start()
    for j in range(steps - 1):
        @pl.when(z > j)
        def _(j=j):
            across(j + 2).start()

    def chosen_copy(d):
        return remote(candidates, chosen, ch_send.at[d - 1], ch_recv, (me, lax.rem(c + d, cands)))

    @pl.when(c == owner_cand)
    def _():
        for d in range(1, cands):
            chosen_copy(d).start()
        chosen[...] = own_candidates[...]

    inverses[y] = grow_inverse(block, small)
    across(0).start()

    @pl.when(y == 0)
    def _():
        across_recv(1).wait_recv()
        beside(1).start()

    points[...] = jnp.transpose(own_candidates[...] * scaling)
    own_points = points[pl.ds(pl.multiple_of(y * half, 8), half), :]
    send_in.wait_send()
    remote(archive, both_archive.at[1 - y], in_send, in_recv, (partner, c)).wait_recv()
    upper_cross = split(matern(own_points, both_archive[0] * scaling))
    lower_cross = split(matern(own_points, both_archive[1] * scaling))

    @pl.when(y == 0)
    def _():
        beside_recv(1).wait_recv()

    coupling = split(jnp.transpose(near[1][:, :height]))
    across_recv(0).wait_recv()
    beside(0).start()
    for j in range(steps - 1):
        @pl.when(z > j)
        def _(j=j):
            far_copy(j).wait()
            across_recv(j + 2).wait_recv()
            beside(j + 2).start()
    beside_recv(0).wait_recv()
    upper = split(inverses[0])
    lower = split(inverses[1])
    between = split(product(coupling, lower))
    first = product(upper_cross, upper)
    second = product(lower_cross, lower) - product(split(first), between)
    columns[y] = jnp.concatenate([first, second], axis=1)

    @pl.when(z > 0)
    def _():
        corner = -product(upper, between)
        whole = split(jnp.concatenate([
            jnp.concatenate([inverses[0], corner], axis=1),
            jnp.concatenate([jnp.zeros((height, height), F32), inverses[1]], axis=1)], axis=0))
        for j in range(steps - 1):
            @pl.when(z > j)
            def _(j=j):
                beside_recv(j + 2).wait_recv()
                weights = product(split(jnp.transpose(far[j].reshape(pair, pair))), whole)
                high, low = split(weights)
                high_weights[j] = high
                low_weights[j] = low

    def onward(j):
        return remote(panels.at[j], panels.at[j], pan_send.at[j], pan_recv.at[j],
                      (lax.rem(me + 2, sections), c))

    for j in range(steps - 1):
        @pl.when(z > j)
        def _(j=j):
            onward(j).wait_recv()
            if j < steps - 2:
                @pl.when(z < steps - 1)
                def _():
                    onward(j).start()
            columns[y] = columns[y] - product(split(panels[j]), (high_weights[j], low_weights[j]))

    def launch(j):
        return remote(columns.at[y], panels.at[j], out_send.at[0], pan_recv.at[j], (lax.rem(me + 2, sections), c))

    for j in range(steps - 1):
        @pl.when(z == j)
        def _(j=j):
            launch(j).start()

    def to_peer(d):
        return remote(columns.at[y], peers.at[c], out_send.at[1 + d], peer_recv.at[c], (me, lax.rem(c + 2 * d, cands)))

    def from_peer(q):
        return remote(columns.at[y], peers.at[q], out_send.at[1], peer_recv.at[q], (me, sibling))

    def pass_on(d):
        q = lax.rem(c + 2 * d, cands)
        return remote(peers.at[q], peers.at[q], pass_send.at[d], peer_recv.at[q], (me, sibling))

    half_count = cands // 2
    for d in range(1, half_count):
        to_peer(d).start()
    to_partner = remote(columns.at[y], columns.at[y], out_send.at[1 + half_count], out_recv, (partner, c))
    to_partner.start()
    to_sibling = remote(columns.at[y], peers.at[c], out_send.at[1], peer_recv.at[c], (me, sibling))
    to_sibling.start()
    peers[c] = columns[y]

    @pl.when(c != owner_cand)
    def _():
        remote(candidates, chosen, ch_send.at[0], ch_recv, (me, sibling)).wait_recv()

    points[...] = jnp.transpose(chosen[...] * scaling)
    within = pl.multiple_of((me * slab) % width, 8)
    covariance[...] = matern(points[pl.ds(within, slab), :], own_candidates[...] * scaling)

    remote(columns.at[y], columns.at[1 - y], out_send.at[1], out_recv, (partner, c)).wait_recv()
    turned[...] = jnp.transpose(columns[...].reshape(width, pair))
    facing = split(turned[...])

    def piece_copy(q):
        group = 2 * q + y
        return remote(pieces.at[q], sums.at[z, group % ratio], sum_send.at[q],
                      sum_recv.at[z, group % ratio], (group // ratio, c))

    def piece(q):
        group = 2 * q + y
        pieces[q] = product(split(peers[q]), facing)

        @pl.when(group // ratio != me)
        def _():
            piece_copy(q).start()

        @pl.when(group // ratio == me)
        def _():
            sums[z, group % ratio] = pieces[q]

    piece(c)
    from_peer(sibling).wait_recv()
    piece(sibling)
    for d in range(1, half_count):
        q = lax.rem(c + 2 * d, cands)
        from_peer(q).wait_recv()
        pass_on(d).start()
        piece(q)
    for d in range(1, half_count):
        q = lax.rem(sibling + 2 * d, cands)
        from_peer(q).wait_recv()
        piece(q)

    whitened[...] = turned[pl.ds(pl.multiple_of(y * height, 8), height), :]

    for k in range(ratio):
        for step in range(steps):
            sender = 2 * step + lax.rem(ratio * me + k, 2)

            @pl.when(sender != me)
            def _(k=k, step=step):
                remote(pieces.at[0], sums.at[step, k], sum_send.at[0], sum_recv.at[step, k], (partner, c)).wait_recv()
        total = functools.reduce(jnp.add, [sums[step, k] for step in range(steps)])
        covariance[k * half:(k + 1) * half] = covariance[k * half:(k + 1) * half] - total

    @pl.when(c == owner_cand)
    def _():
        for d in range(1, cands):
            chosen_copy(d).wait_send()
    across(0).wait_send()
    beside(0).wait_send()

    @pl.when(y == 1)
    def _():
        across(1).wait_send()

    @pl.when(y == 0)
    def _():
        beside(1).wait_send()
    for j in range(steps - 1):
        @pl.when(z > j)
        def _(j=j):
            across(j + 2).wait_send()
            beside(j + 2).wait_send()
            if j < steps - 2:
                @pl.when(z < steps - 1)
                def _():
                    onward(j).wait_send()

        @pl.when(z == j)
        def _(j=j):
            launch(j).wait_send()
    for d in range(1, half_count):
        to_peer(d).wait_send()
        pass_on(d).wait_send()
    to_sibling.wait_send()
    to_partner.wait_send()
    for q in range(cands):
        @pl.when((2 * q + y) // ratio != me)
        def _(q=q):
            piece_copy(q).wait_send()


def shards(sections, cands, archive, candidates, lengths, factor):
    dims, height = archive.shape
    width = candidates.shape[1]
    pair, half, steps = 2 * height, width // 2, sections // 2
    ratio = (2 * cands) // sections
    vmem = pl.BlockSpec(memory_space=pltpu.VMEM)
    hbm = pl.BlockSpec(memory_space=pltpu.HBM)
    dma = pltpu.SemaphoreType.DMA
    return pl.pallas_call(
        functools.partial(kernel, sections, cands),
        out_shape=(jax.ShapeDtypeStruct((height, width), F32), jax.ShapeDtypeStruct((half * ratio, width), F32)),
        in_specs=[hbm] * 4,
        out_specs=(vmem, vmem),
        scratch_shapes=[
            pltpu.VMEM((2, dims, height), F32),
            pltpu.VMEM((2, height, pair), F32),
            pltpu.VMEM((steps - 1, 2, height, pair), F32),
            pltpu.VMEM((dims, width), F32),
            pltpu.VMEM((1, dims), F32),
            pltpu.VMEM((dims, width), F32),
            pltpu.VMEM((width, dims), F32),
            pltpu.VMEM((2, height, height), F32),
            pltpu.VMEM((steps - 1, pair, pair), jnp.bfloat16),
            pltpu.VMEM((steps - 1, pair, pair), jnp.bfloat16),
            pltpu.VMEM((steps - 1, half, pair), F32),
            pltpu.VMEM((cands, half, pair), F32),
            pltpu.VMEM((2, half, pair), F32),
            pltpu.VMEM((pair, width), F32),
            pltpu.VMEM((steps, ratio, half, width), F32),
            pltpu.VMEM((cands, half, width), F32),
            dma((4,)), dma((steps - 1,)),
            dma, dma,
            dma((cands - 1,)), dma,
            dma((steps + 1,)), dma((steps + 1,)), dma((steps + 1,)), dma((steps + 1,)),
            dma((steps - 1,)), dma((steps - 1,)),
            dma((2 + cands // 2,)), dma,
            dma((cands // 2,)), dma((cands,)),
            dma((cands,)), dma((steps, ratio)),
        ],
        compiler_params=pltpu.CompilerParams(
            collective_id=0, has_side_effects=True, vmem_limit_bytes=62 * 1024 * 1024),
    )(archive, candidates, lengths.reshape(1, dims), factor)


def solution(mesh):
    return jax.shard_map(
        functools.partial(shards, mesh.shape["chain"], mesh.shape["cand"]),
        mesh=mesh,
        in_specs=(P(None, "chain"), P(None, "cand"), P(), P("chain", None)),
        out_specs=(P("chain", "cand"), P("chain", "cand")),
        check_vma=False,
    )
```

time: 47.6 us -> 44.4 us (0.933)
  the two profiles are of different devices: /device:TPU:0 before, /device:TPU:7 now
where the time goes in v2:
time: 44.4 us; the launch traced here: 44.1 us
  Pallas kernels  40.6 us (91%)
  local copies, waits for them, and re-layouts  2.91 us (7%)
  between operations  0.64 us (1%)
    pallas_call x1, Pallas kernels, shards(): pl.pallas_call(functools.partial(kernel, sections, cands), out_shape=(jax...  40.6 us
    unnamed x2, local copies, waits for them, and re-layouts  2.91 us

profile of v2, /device:TPU:7, one launch (start us, length us, event | category | flops | bytes accessed | tf_op | source)
XLA Modules:
  0.0 44.1 jit_solution(2937974164583095976)
XLA Ops:
  0.6 40.6 %shard_map.59 = (f32[192,128]{1,0:T(8,128)}, f32[64,128]{1,0:T(8,128)}) custom-call(f32[32,192]{1,0:T(8,128)} %archive.1, f32[32,128]{1,0:T(8,128)} %candidates.1, f32[1,32]{1,0:T(1,128)} %bitcast.1, f32[192,1536]{1,0:T(8,128)} %factor.1), custom_call_target="tpu_custom_call" | custom-call | tf_op jit(solution)/shard_map/pallas_call | solution.py:376
  41.2 1.5 %copy.8 = f32[192,128]{1,0:T(8,128)} copy(f32[192,128]{1,0:T(8,128)} %get-tuple-element.4) | data formatting | bytes 196608
  42.8 1.4 %copy.9 = f32[64,128]{1,0:T(8,128)} copy(f32[64,128]{1,0:T(8,128)} %get-tuple-element.5) | data formatting | bytes 65536

commit v3 on v2

--- a/solution.py
+++ b/solution.py
@@ -8,7 +8,7 @@
 
 MESH = pl.DeviceIdType.MESH
 F32 = jnp.float32
-BASE = 16
+BASE = 32
 
 
 def split(value):
@@ -58,12 +58,12 @@
     return jnp.where(same, jnp.concatenate([state] * count, axis=0), 0.0)
 
 
-def grow_inverse(block, inverse):
+def grow_inverse(block, inverse, start, end):
     size = block.shape[0]
     row = lax.broadcasted_iota(jnp.int32, (size, size), 0)
     column = lax.broadcasted_iota(jnp.int32, (size, size), 1)
-    width = BASE
-    while width < size:
+    width = start
+    while width < end:
         above = ((row // width) + 1 == (column // width)) & ((row // (2 * width)) == (column // (2 * width)))
         parts = split(inverse)
         middle = product(parts, split(jnp.where(above, block, 0.0)))
@@ -127,6 +127,7 @@
     block = jnp.where(y == 0, strip_of_pair[:, :height], strip_of_pair[:, height:])
     small = jnp.transpose(base_inverse(block))
     block = jnp.transpose(block)
+    small = grow_inverse(block, small, BASE, 2 * BASE)
     lengths_copy.wait()
     candidates_copy.wait()
     archive_copy.wait()
@@ -167,7 +168,8 @@
     @pl.when(y == 1)
     def _():
         across(1).start()
-    for j in range(steps - 1):
+    early = min(2, steps - 1)
+    for j in range(early):
         @pl.when(z > j)
         def _(j=j):
             across(j + 2).start()
@@ -181,8 +183,12 @@
             chosen_copy(d).start()
         chosen[...] = own_candidates[...]
 
-    inverses[y] = grow_inverse(block, small)
+    inverses[y] = grow_inverse(block, small, 2 * BASE, height)
     across(0).start()
+    for j in range(early, steps - 1):
+        @pl.when(z > j)
+        def _(j=j):
+            across(j + 2).start()
 
     @pl.when(y == 0)
     def _():
@@ -201,14 +207,28 @@
         beside_recv(1).wait_recv()
 
     coupling = split(jnp.transpose(near[1][:, :height]))
+
+    def pass_far(j):
+        far_copy(j).wait()
+        across_recv(j + 2).wait_recv()
+        beside(j + 2).start()
+
+    def turn_far(j):
+        beside_recv(j + 2).wait_recv()
+        high, low = split(jnp.transpose(far[j].reshape(pair, pair)))
+        high_weights[j] = high
+        low_weights[j] = low
+
+    for j in range(early):
+        @pl.when(z > j)
+        def _(j=j):
+            pass_far(j)
     across_recv(0).wait_recv()
     beside(0).start()
-    for j in range(steps - 1):
-        @pl.when(z > j)
-        def _(j=j):
-            far_copy(j).wait()
-            across_recv(j + 2).wait_recv()
-            beside(j + 2).start()
+    for j in range(early):
+        @pl.when(z > j)
+        def _(j=j):
+            turn_far(j)
     beside_recv(0).wait_recv()
     upper = split(inverses[0])
     lower = split(inverses[1])
@@ -226,8 +246,10 @@
         for j in range(steps - 1):
             @pl.when(z > j)
             def _(j=j):
-                beside_recv(j + 2).wait_recv()
-                weights = product(split(jnp.transpose(far[j].reshape(pair, pair))), whole)
+                if j >= early:
+                    pass_far(j)
+                    turn_far(j)
+                weights = product((high_weights[j], low_weights[j]), whole)
                 high, low = split(weights)
                 high_weights[j] = high
                 low_weights[j] = low
@@ -281,6 +303,9 @@
     within = pl.multiple_of((me * slab) % width, 8)
     covariance[...] = matern(points[pl.ds(within, slab), :], own_candidates[...] * scaling)
 
+    for d in range(1, half_count):
+        from_peer(lax.rem(c + 2 * d, cands)).wait_recv()
+        pass_on(d).start()
     remote(columns.at[y], columns.at[1 - y], out_send.at[1], out_recv, (partner, c)).wait_recv()
     turned[...] = jnp.transpose(columns[...].reshape(width, pair))
     facing = split(turned[...])
@@ -306,10 +331,7 @@
     from_peer(sibling).wait_recv()
     piece(sibling)
     for d in range(1, half_count):
-        q = lax.rem(c + 2 * d, cands)
-        from_peer(q).wait_recv()
-        pass_on(d).start()
-        piece(q)
+        piece(lax.rem(c + 2 * d, cands))
     for d in range(1, half_count):
         q = lax.rem(sibling + 2 * d, cands)
         from_peer(q).wait_recv()
@@ -405,8 +427,9 @@
             dma((cands,)), dma((steps, ratio)),
         ],
         compiler_params=pltpu.CompilerParams(
-            collective_id=0, has_side_effects=True, vmem_limit_bytes=62 * 1024 * 1024),
-    )(archive, candidates, lengths.reshape(1, dims), factor)
+            collective_id=0, has_side_effects=True, vmem_limit_bytes=48 * 1024 * 1024),
+    )(*(pltpu.with_memory_space_constraint(x, pltpu.HBM)
+        for x in (archive, candidates, lengths.reshape(1, dims), factor)))
 
 
 def solution(mesh):

time: 44.4 us -> 43.5 us (0.980)
  the two profiles are of different devices: /device:TPU:7 before, /device:TPU:0 now
where the time goes in v3:
time: 43.5 us; the launch traced here: 43.3 us
  Pallas kernels  41.4 us (95%)
  local copies, waits for them, and re-layouts  1.26 us (3%)
  between operations  0.64 us (1%)
    pallas_call x1, Pallas kernels, shards(): pl.pallas_call(functools.partial(kernel, sections, cands), out_shape=(jax...  41.4 us
    unnamed x2, local copies, waits for them, and re-layouts  1.26 us

profile of v3, /device:TPU:0, one launch (start us, length us, event | category | flops | bytes accessed | tf_op | source)
XLA Modules:
  0.0 43.3 jit_solution(127608440874808754)
XLA Ops:
  0.6 41.4 %shard_map.59 = (f32[192,128]{1,0:T(8,128)S(1)}, f32[64,128]{1,0:T(8,128)S(1)}) custom-call(f32[32,192]{1,0:T(8,128)} %archive.1, f32[32,128]{1,0:T(8,128)} %candidates.1, f32[1,32]{1,0:T(1,128)} %bitcast.1, f32[192,1536]{1,0:T(8,128)} %factor.1), custom_call_target="tpu_custom_call" | custom-call | tf_op jit(solution)/shard_map/pallas_call | solution.py:398
  42.1 0.6 %copy.8 = f32[192,128]{1,0:T(8,128)} copy(f32[192,128]{1,0:T(8,128)S(1)} %get-tuple-element.4) | data formatting | bytes 196608
  42.7 0.6 %copy.9 = f32[64,128]{1,0:T(8,128)} copy(f32[64,128]{1,0:T(8,128)S(1)} %get-tuple-element.5) | data formatting | bytes 65536

commit v4 on v3

--- a/solution.py
+++ b/solution.py
@@ -9,6 +9,8 @@
 MESH = pl.DeviceIdType.MESH
 F32 = jnp.float32
 BASE = 32
+TILE = 128
+CHUNKS = 2
 
 
 def split(value):
@@ -72,6 +74,20 @@
     return inverse
 
 
+def pack(upper):
+    size = upper.shape[0]
+    rest = upper[:, TILE:]
+    beside = jnp.concatenate([rest[:size // 2], rest[size // 2:]], axis=1)
+    return jnp.concatenate([upper[:TILE, :TILE], beside], axis=0)
+
+
+def unpack(packed, size):
+    beside = packed[TILE:]
+    rest = jnp.concatenate([beside[:, :size - TILE], beside[:, size - TILE:]], axis=0)
+    first = jnp.concatenate([packed[:TILE], jnp.zeros((size - TILE, TILE), F32)], axis=0)
+    return jnp.concatenate([first, rest], axis=1)
+
+
 def kernel(sections, cands, archive, candidates, lengths, factor, whitened, covariance,
            both_archive, near, far, own_candidates, own_lengths, chosen, points, inverses,
            high_weights, low_weights, panels, peers, columns, turned, sums, pieces,
@@ -141,22 +157,22 @@
     send_in.start()
 
     def area(e, who, rows):
-        if e == 0:
-            return inverses.at[who, rows]
         if e == 1:
             return near.at[1, rows, pl.ds(0, cover)]
         return far.at[e - 2, who, rows]
 
     def across(e):
         if e == 0:
-            source = inverses.at[y, mine]
-        elif e == 1:
+            return remote(inverses.at[y], inverses.at[y], y_send.at[e], y_recv.at[e], (partner, c))
+        if e == 1:
             source = factor.at[mine, pl.ds(diagonal, cover)]
         else:
             source = factor.at[mine, pl.ds((e - 2) * pair, pair)]
         return remote(source, area(e, y, mine), y_send.at[e], y_recv.at[e], (partner, c))
 
     def across_recv(e):
+        if e == 0:
+            return remote(inverses.at[1 - y], inverses.at[1 - y], y_send.at[e], y_recv.at[e], (partner, c))
         return remote(area(e, 1 - y, mine), area(e, 1 - y, mine), y_send.at[e], y_recv.at[e], (partner, c))
 
     def beside(e):
@@ -183,7 +199,7 @@
             chosen_copy(d).start()
         chosen[...] = own_candidates[...]
 
-    inverses[y] = grow_inverse(block, small, 2 * BASE, height)
+    inverses[y] = pack(grow_inverse(block, small, 2 * BASE, height))
     across(0).start()
     for j in range(early, steps - 1):
         @pl.when(z > j)
@@ -223,26 +239,62 @@
         @pl.when(z > j)
         def _(j=j):
             pass_far(j)
+    for j in range(early):
+        @pl.when(z > j)
+        def _(j=j):
+            turn_far(j)
     across_recv(0).wait_recv()
-    beside(0).start()
-    for j in range(early):
-        @pl.when(z > j)
-        def _(j=j):
-            turn_far(j)
-    beside_recv(0).wait_recv()
-    upper = split(inverses[0])
-    lower = split(inverses[1])
+    upper_inverse = unpack(inverses[0], height)
+    lower_inverse = unpack(inverses[1], height)
+    upper = split(upper_inverse)
+    lower = split(lower_inverse)
     between = split(product(coupling, lower))
-    first = product(upper_cross, upper)
-    second = product(lower_cross, lower) - product(split(first), between)
-    columns[y] = jnp.concatenate([first, second], axis=1)
+    part = half // CHUNKS
+    half_count = cands // 2
+
+    def rows_of(k):
+        return pl.ds(k * part, part)
+
+    def launch(j, k):
+        return remote(columns.at[y, rows_of(k)], panels.at[j, rows_of(k)], out_send.at[0, k], pan_recv.at[j, k],
+                      (lax.rem(me + 2, sections), c))
+
+    def to_peer(d, k):
+        return remote(columns.at[y, rows_of(k)], peers.at[c, rows_of(k)], out_send.at[1 + d, k], peer_recv.at[c, k],
+                      (me, lax.rem(c + 2 * d, cands)))
+
+    def to_sibling(k):
+        return remote(columns.at[y, rows_of(k)], peers.at[c, rows_of(k)], out_send.at[1, k], peer_recv.at[c, k],
+                      (me, sibling))
+
+    def to_partner(k):
+        return remote(columns.at[y, rows_of(k)], columns.at[y, rows_of(k)], out_send.at[1 + half_count, k],
+                      out_recv.at[k], (partner, c))
+
+    def emit(j, k):
+        if j < steps - 1:
+            launch(j, k).start()
+        for d in range(1, half_count):
+            to_peer(d, k).start()
+        to_partner(k).start()
+        to_sibling(k).start()
+
+    for k in range(CHUNKS):
+        rows = slice(k * part, (k + 1) * part)
+        first = product([p[rows] for p in upper_cross], upper)
+        second = product([p[rows] for p in lower_cross], lower) - product(split(first), between)
+        columns[y, rows] = jnp.concatenate([first, second], axis=1)
+
+        @pl.when(z == 0)
+        def _(k=k):
+            emit(0, k)
 
     @pl.when(z > 0)
     def _():
         corner = -product(upper, between)
         whole = split(jnp.concatenate([
-            jnp.concatenate([inverses[0], corner], axis=1),
-            jnp.concatenate([jnp.zeros((height, height), F32), inverses[1]], axis=1)], axis=0))
+            jnp.concatenate([upper_inverse, corner], axis=1),
+            jnp.concatenate([jnp.zeros((height, height), F32), lower_inverse], axis=1)], axis=0))
         for j in range(steps - 1):
             @pl.when(z > j)
             def _(j=j):
@@ -254,45 +306,40 @@
                 high_weights[j] = high
                 low_weights[j] = low
 
-    def onward(j):
-        return remote(panels.at[j], panels.at[j], pan_send.at[j], pan_recv.at[j],
+    def onward(j, k):
+        return remote(panels.at[j, rows_of(k)], panels.at[j, rows_of(k)], pan_send.at[j, k], pan_recv.at[j, k],
                       (lax.rem(me + 2, sections), c))
 
     for j in range(steps - 1):
         @pl.when(z > j)
         def _(j=j):
-            onward(j).wait_recv()
-            if j < steps - 2:
-                @pl.when(z < steps - 1)
+            for k in range(CHUNKS):
+                onward(j, k).wait_recv()
+                if j < steps - 2:
+                    @pl.when(z < steps - 1)
+                    def _():
+                        onward(j, k).start()
+                rows = slice(k * part, (k + 1) * part)
+                columns[y, rows] = columns[y, rows] - product(
+                    split(panels[j, rows]), (high_weights[j], low_weights[j]))
+
+                @pl.when(z == j + 1)
                 def _():
-                    onward(j).start()
-            columns[y] = columns[y] - product(split(panels[j]), (high_weights[j], low_weights[j]))
-
-    def launch(j):
-        return remote(columns.at[y], panels.at[j], out_send.at[0], pan_recv.at[j], (lax.rem(me + 2, sections), c))
-
-    for j in range(steps - 1):
-        @pl.when(z == j)
-        def _(j=j):
-            launch(j).start()
-
-    def to_peer(d):
-        return remote(columns.at[y], peers.at[c], out_send.at[1 + d], peer_recv.at[c], (me, lax.rem(c + 2 * d, cands)))
-
-    def from_peer(q):
-        return remote(columns.at[y], peers.at[q], out_send.at[1], peer_recv.at[q], (me, sibling))
-
-    def pass_on(d):
+                    emit(j + 1, k)
+
+    def from_peer(q, k):
+        return remote(columns.at[y, rows_of(k)], peers.at[q, rows_of(k)], out_send.at[1, k], peer_recv.at[q, k],
+                      (me, sibling))
+
+    def pass_on(d, k):
         q = lax.rem(c + 2 * d, cands)
-        return remote(peers.at[q], peers.at[q], pass_send.at[d], peer_recv.at[q], (me, sibling))
-
-    half_count = cands // 2
-    for d in range(1, half_count):
-        to_peer(d).start()
-    to_partner = remote(columns.at[y], columns.at[y], out_send.at[1 + half_count], out_recv, (partner, c))
-    to_partner.start()
-    to_sibling = remote(columns.at[y], peers.at[c], out_send.at[1], peer_recv.at[c], (me, sibling))
-    to_sibling.start()
+        return remote(peers.at[q, rows_of(k)], peers.at[q, rows_of(k)], pass_send.at[d, k], peer_recv.at[q, k],
+                      (me, sibling))
+
+    def wait_peer(q):
+        for k in range(CHUNKS):
+            from_peer(q, k).wait_recv()
+
     peers[c] = columns[y]
 
     @pl.when(c != owner_cand)
@@ -303,10 +350,13 @@
     within = pl.multiple_of((me * slab) % width, 8)
     covariance[...] = matern(points[pl.ds(within, slab), :], own_candidates[...] * scaling)
 
-    for d in range(1, half_count):
-        from_peer(lax.rem(c + 2 * d, cands)).wait_recv()
-        pass_on(d).start()
-    remote(columns.at[y], columns.at[1 - y], out_send.at[1], out_recv, (partner, c)).wait_recv()
+    for k in range(CHUNKS):
+        for d in range(1, half_count):
+            from_peer(lax.rem(c + 2 * d, cands), k).wait_recv()
+            pass_on(d, k).start()
+    for k in range(CHUNKS):
+        remote(columns.at[y, rows_of(k)], columns.at[1 - y, rows_of(k)], out_send.at[1, k], out_recv.at[k],
+               (partner, c)).wait_recv()
     turned[...] = jnp.transpose(columns[...].reshape(width, pair))
     facing = split(turned[...])
 
@@ -328,13 +378,13 @@
             sums[z, group % ratio] = pieces[q]
 
     piece(c)
-    from_peer(sibling).wait_recv()
+    wait_peer(sibling)
     piece(sibling)
     for d in range(1, half_count):
         piece(lax.rem(c + 2 * d, cands))
     for d in range(1, half_count):
         q = lax.rem(sibling + 2 * d, cands)
-        from_peer(q).wait_recv()
+        wait_peer(q)
         piece(q)
 
     whitened[...] = turned[pl.ds(pl.multiple_of(y * height, 8), height), :]
@@ -354,7 +404,6 @@
         for d in range(1, cands):
             chosen_copy(d).wait_send()
     across(0).wait_send()
-    beside(0).wait_send()
 
     @pl.when(y == 1)
     def _():
@@ -371,16 +420,19 @@
             if j < steps - 2:
                 @pl.when(z < steps - 1)
                 def _():
-                    onward(j).wait_send()
+                    for k in range(CHUNKS):
+                        onward(j, k).wait_send()
 
         @pl.when(z == j)
         def _(j=j):
-            launch(j).wait_send()
-    for d in range(1, half_count):
-        to_peer(d).wait_send()
-        pass_on(d).wait_send()
-    to_sibling.wait_send()
-    to_partner.wait_send()
+            for k in range(CHUNKS):
+                launch(j, k).wait_send()
+    for k in range(CHUNKS):
+        for d in range(1, half_count):
+            to_peer(d, k).wait_send()
+            pass_on(d, k).wait_send()
+        to_sibling(k).wait_send()
+        to_partner(k).wait_send()
     for q in range(cands):
         @pl.when((2 * q + y) // ratio != me)
         def _(q=q):
@@ -408,7 +460,7 @@
             pltpu.VMEM((1, dims), F32),
             pltpu.VMEM((dims, width), F32),
             pltpu.VMEM((width, dims), F32),
-            pltpu.VMEM((2, height, height), F32),
+            pltpu.VMEM((2, TILE + height // 2, TILE), F32),
             pltpu.VMEM((steps - 1, pair, pair), jnp.bfloat16),
             pltpu.VMEM((steps - 1, pair, pair), jnp.bfloat16),
             pltpu.VMEM((steps - 1, half, pair), F32),
@@ -421,9 +473,9 @@
             dma, dma,
             dma((cands - 1,)), dma,
             dma((steps + 1,)), dma((steps + 1,)), dma((steps + 1,)), dma((steps + 1,)),
-            dma((steps - 1,)), dma((steps - 1,)),
-            dma((2 + cands // 2,)), dma,
-            dma((cands // 2,)), dma((cands,)),
+            dma((steps - 1, CHUNKS)), dma((steps - 1, CHUNKS)),
+            dma((2 + cands // 2, CHUNKS)), dma((CHUNKS,)),
+            dma((cands // 2, CHUNKS)), dma((cands, CHUNKS)),
             dma((cands,)), dma((steps, ratio)),
         ],
         compiler_params=pltpu.CompilerParams(

time: 43.5 us -> 42.3 us (0.972)
  Pallas kernels: 41.4 us -> 40.2 us
    pallas_call x1, Pallas kernels: 41.4 us -> 40.2 us  [shards(): pl.pallas_call(functools.partial(kernel, sections, cands), out_shape=(jax...]
where the time goes in v4:
time: 42.3 us; the launch traced here: 42.1 us
  Pallas kernels  40.2 us (95%)
  local copies, waits for them, and re-layouts  1.26 us (3%)
  between operations  0.64 us (2%)
    pallas_call x1, Pallas kernels, shards(): pl.pallas_call(functools.partial(kernel, sections, cands), out_shape=(jax...  40.2 us
    unnamed x2, local copies, waits for them, and re-layouts  1.26 us

profile of v4, /device:TPU:0, one launch (start us, length us, event | category | flops | bytes accessed | tf_op | source)
XLA Modules:
  0.0 42.1 jit_solution(2398508152088998848)
XLA Ops:
  0.6 40.2 %shard_map.59 = (f32[192,128]{1,0:T(8,128)S(1)}, f32[64,128]{1,0:T(8,128)S(1)}) custom-call(f32[32,192]{1,0:T(8,128)} %archive.1, f32[32,128]{1,0:T(8,128)} %candidates.1, f32[1,32]{1,0:T(1,128)} %bitcast.1, f32[192,1536]{1,0:T(8,128)} %factor.1), custom_call_target="tpu_custom_call" | custom-call | tf_op jit(solution)/shard_map/pallas_call | solution.py:450
  40.9 0.6 %copy.8 = f32[192,128]{1,0:T(8,128)} copy(f32[192,128]{1,0:T(8,128)S(1)} %get-tuple-element.4) | data formatting | bytes 196608
  41.5 0.6 %copy.9 = f32[64,128]{1,0:T(8,128)} copy(f32[64,128]{1,0:T(8,128)S(1)} %get-tuple-element.5) | data formatting | bytes 65536

commit v5 on v4

--- a/solution.py
+++ b/solution.py
@@ -92,7 +92,7 @@
            both_archive, near, far, own_candidates, own_lengths, chosen, points, inverses,
            high_weights, low_weights, panels, peers, columns, turned, sums, pieces,
            load, far_load, in_send, in_recv, ch_send, ch_recv, y_send, y_recv, s_send, s_recv,
-           pan_send, pan_recv, out_send, out_recv, pass_send, peer_recv, sum_send, sum_recv):
+           pan_send, pan_recv, out_send, out_recv, pass_send, peer_recv, sum_send, sum_recv, ready):
     me = lax.axis_index("chain")
     c = lax.axis_index("cand")
     z, y = me // 2, me % 2
@@ -129,8 +129,15 @@
     archive_copy.start()
 
     barrier = pltpu.get_barrier_semaphore()
-    for d in range(1, sections):
-        pl.semaphore_signal(barrier, inc=1, device_id=(lax.rem(me + d, sections), c), device_id_type=MESH)
+    pl.semaphore_signal(barrier, inc=1, device_id=(partner, c), device_id_type=MESH)
+
+    @pl.when(z > 0)
+    def _():
+        pl.semaphore_signal(barrier, inc=1, device_id=(lax.rem(me + sections - 2, sections), c), device_id_type=MESH)
+
+    @pl.when(z < steps - 1)
+    def _():
+        pl.semaphore_signal(barrier, inc=1, device_id=(lax.rem(me + 2, sections), c), device_id_type=MESH)
     for d in range(1, cands):
         pl.semaphore_signal(barrier, inc=1, device_id=(me, lax.rem(c + d, cands)), device_id_type=MESH)
     for j in range(steps - 1):
@@ -151,7 +158,8 @@
     scaling = jnp.transpose(jnp.broadcast_to(scale_row, (8, scale_row.shape[1])))[:, :1]
     owner_cand = (me * slab) // width
 
-    pl.semaphore_wait(barrier, sections + cands - 2)
+    neighbours = cands + jnp.where(z > 0, 1, 0) + jnp.where(z < steps - 1, 1, 0)
+    pl.semaphore_wait(barrier, neighbours)
 
     send_in = remote(archive, both_archive.at[y], in_send, in_recv, (partner, c))
     send_in.start()
@@ -215,8 +223,9 @@
     own_points = points[pl.ds(pl.multiple_of(y * half, 8), half), :]
     send_in.wait_send()
     remote(archive, both_archive.at[1 - y], in_send, in_recv, (partner, c)).wait_recv()
-    upper_cross = split(matern(own_points, both_archive[0] * scaling))
-    lower_cross = split(matern(own_points, both_archive[1] * scaling))
+    cross = jnp.concatenate(
+        [matern(own_points, both_archive[0] * scaling), matern(own_points, both_archive[1] * scaling)], axis=1)
+    columns[y] = cross
 
     @pl.when(y == 0)
     def _():
@@ -243,6 +252,14 @@
         @pl.when(z > j)
         def _(j=j):
             turn_far(j)
+    @pl.when((z > 0) & (z < steps - 1))
+    def _():
+        pl.semaphore_wait(ready, 1)
+
+    @pl.when(z > 0)
+    def _():
+        pl.semaphore_signal(ready, inc=1, device_id=(lax.rem(me + sections - 2, sections), c), device_id_type=MESH)
+
     across_recv(0).wait_recv()
     upper_inverse = unpack(inverses[0], height)
     lower_inverse = unpack(inverses[1], height)
@@ -279,15 +296,31 @@
         to_partner(k).start()
         to_sibling(k).start()
 
-    for k in range(CHUNKS):
+    def solve(k):
         rows = slice(k * part, (k + 1) * part)
-        first = product([p[rows] for p in upper_cross], upper)
-        second = product([p[rows] for p in lower_cross], lower) - product(split(first), between)
+        residue = columns[y, rows]
+        first = product(split(residue[:, :height]), upper)
+        second = product(split(residue[:, height:]), lower) - product(split(first), between)
         columns[y, rows] = jnp.concatenate([first, second], axis=1)
 
-        @pl.when(z == 0)
-        def _(k=k):
+    @pl.when(z == 0)
+    def _():
+        for k in range(CHUNKS):
+            solve(k)
             emit(0, k)
+
+    def onward(j, k):
+        return remote(panels.at[j, rows_of(k)], panels.at[j, rows_of(k)], pan_send.at[j, k], pan_recv.at[j, k],
+                      (lax.rem(me + 2, sections), c))
+
+    def subtract(j, k, weights):
+        onward(j, k).wait_recv()
+        if j < steps - 2:
+            @pl.when(z < steps - 1)
+            def _():
+                onward(j, k).start()
+        rows = slice(k * part, (k + 1) * part)
+        columns[y, rows] = columns[y, rows] - product(split(panels[j, rows]), weights)
 
     @pl.when(z > 0)
     def _():
@@ -295,36 +328,29 @@
         whole = split(jnp.concatenate([
             jnp.concatenate([upper_inverse, corner], axis=1),
             jnp.concatenate([jnp.zeros((height, height), F32), lower_inverse], axis=1)], axis=0))
-        for j in range(steps - 1):
+        for j in range(early, steps - 1):
             @pl.when(z > j)
             def _(j=j):
-                if j >= early:
-                    pass_far(j)
-                    turn_far(j)
-                weights = product((high_weights[j], low_weights[j]), whole)
-                high, low = split(weights)
+                pass_far(j)
+                turn_far(j)
+        for j in range(steps - 1):
+            @pl.when(z == j + 1)
+            def _(j=j):
+                high, low = split(product((high_weights[j], low_weights[j]), whole))
                 high_weights[j] = high
                 low_weights[j] = low
-
-    def onward(j, k):
-        return remote(panels.at[j, rows_of(k)], panels.at[j, rows_of(k)], pan_send.at[j, k], pan_recv.at[j, k],
-                      (lax.rem(me + 2, sections), c))
-
-    for j in range(steps - 1):
-        @pl.when(z > j)
-        def _(j=j):
-            for k in range(CHUNKS):
-                onward(j, k).wait_recv()
-                if j < steps - 2:
-                    @pl.when(z < steps - 1)
-                    def _():
-                        onward(j, k).start()
-                rows = slice(k * part, (k + 1) * part)
-                columns[y, rows] = columns[y, rows] - product(
-                    split(panels[j, rows]), (high_weights[j], low_weights[j]))
-
-                @pl.when(z == j + 1)
-                def _():
+        for j in range(steps - 2):
+            @pl.when(z > j + 1)
+            def _(j=j):
+                for k in range(CHUNKS):
+                    subtract(j, k, (high_weights[j], low_weights[j]))
+        for k in range(CHUNKS):
+            solve(k)
+        for j in range(steps - 1):
+            @pl.when(z == j + 1)
+            def _(j=j):
+                for k in range(CHUNKS):
+                    subtract(j, k, (high_weights[j], low_weights[j]))
                     emit(j + 1, k)
 
     def from_peer(q, k):
@@ -376,6 +402,10 @@
         @pl.when(group // ratio == me)
         def _():
             sums[z, group % ratio] = pieces[q]
+
+    @pl.when(z == 0)
+    def _():
+        pl.semaphore_wait(ready, 1)
 
     piece(c)
     wait_peer(sibling)
@@ -477,6 +507,7 @@
             dma((2 + cands // 2, CHUNKS)), dma((CHUNKS,)),
             dma((cands // 2, CHUNKS)), dma((cands, CHUNKS)),
             dma((cands,)), dma((steps, ratio)),
+            pltpu.SemaphoreType.REGULAR,
         ],
         compiler_params=pltpu.CompilerParams(
             collective_id=0, has_side_effects=True, vmem_limit_bytes=48 * 1024 * 1024),

time: 42.3 us -> 48.2 us (1.14)
  Pallas kernels: 40.2 us -> 46.1 us
    pallas_call x1, Pallas kernels: 40.2 us -> 46.1 us  [shards(): pl.pallas_call(functools.partial(kernel, sections, cands), out_shape=(jax...]
where the time goes in v5:
time: 48.2 us; the launch traced here: 48 us
  Pallas kernels  46.1 us (96%)
  local copies, waits for them, and re-layouts  1.26 us (3%)
  between operations  0.64 us (1%)
    pallas_call x1, Pallas kernels, shards(): pl.pallas_call(functools.partial(kernel, sections, cands), out_shape=(jax...  46.1 us
    unnamed x2, local copies, waits for them, and re-layouts  1.26 us

profile of v5, /device:TPU:0, one launch (start us, length us, event | category | flops | bytes accessed | tf_op | source)
XLA Modules:
  0.0 48.0 jit_solution(6999653452918191813)
XLA Ops:
  0.6 46.1 %shard_map.59 = (f32[192,128]{1,0:T(8,128)S(1)}, f32[64,128]{1,0:T(8,128)S(1)}) custom-call(f32[32,192]{1,0:T(8,128)} %archive.1, f32[32,128]{1,0:T(8,128)} %candidates.1, f32[1,32]{1,0:T(1,128)} %bitcast.1, f32[192,1536]{1,0:T(8,128)} %factor.1), custom_call_target="tpu_custom_call" | custom-call | tf_op jit(solution)/shard_map/pallas_call | solution.py:480
  46.8 0.6 %copy.8 = f32[192,128]{1,0:T(8,128)} copy(f32[192,128]{1,0:T(8,128)S(1)} %get-tuple-element.4) | data formatting | bytes 196608
  47.4 0.6 %copy.9 = f32[64,128]{1,0:T(8,128)} copy(f32[64,128]{1,0:T(8,128)S(1)} %get-tuple-element.5) | data formatting | bytes 65536

commit v6 on v5

--- a/solution.py
+++ b/solution.py
@@ -21,7 +21,9 @@
 def product(first, second, transposed=False):
     dims = (((1,), (1 if transposed else 0,)), ((), ()))
     dot = functools.partial(lax.dot_general, dimension_numbers=dims, preferred_element_type=F32)
-    return dot(first[0], second[0]) + (dot(first[0], second[1]) + dot(first[1], second[0]))
+    count = first[0].shape[0]
+    stacked = dot(jnp.concatenate([first[0], first[1]], axis=0), second[0])
+    return stacked[:count] + (stacked[count:] + dot(first[0], second[1]))
 
 
 def matern(rows, columns):
@@ -328,30 +330,26 @@
         whole = split(jnp.concatenate([
             jnp.concatenate([upper_inverse, corner], axis=1),
             jnp.concatenate([jnp.zeros((height, height), F32), lower_inverse], axis=1)], axis=0))
-        for j in range(early, steps - 1):
+        for j in range(steps - 1):
             @pl.when(z > j)
             def _(j=j):
-                pass_far(j)
-                turn_far(j)
-        for j in range(steps - 1):
-            @pl.when(z == j + 1)
-            def _(j=j):
+                if j >= early:
+                    pass_far(j)
+                    turn_far(j)
                 high, low = split(product((high_weights[j], low_weights[j]), whole))
                 high_weights[j] = high
                 low_weights[j] = low
-        for j in range(steps - 2):
-            @pl.when(z > j + 1)
+            if j == 0:
+                columns[y] = product(split(columns[y]), whole)
+        for j in range(steps - 1):
+            @pl.when(z > j)
             def _(j=j):
                 for k in range(CHUNKS):
                     subtract(j, k, (high_weights[j], low_weights[j]))
-        for k in range(CHUNKS):
-            solve(k)
-        for j in range(steps - 1):
-            @pl.when(z == j + 1)
-            def _(j=j):
-                for k in range(CHUNKS):
-                    subtract(j, k, (high_weights[j], low_weights[j]))
-                    emit(j + 1, k)
+
+                    @pl.when(z == j + 1)
+                    def _():
+                        emit(j + 1, k)
 
     def from_peer(q, k):
         return remote(columns.at[y, rows_of(k)], peers.at[q, rows_of(k)], out_send.at[1, k], peer_recv.at[q, k],

time: 48.2 us -> 47.7 us (0.990)
  no operation moved by 1% of the time
where the time goes in v6:
time: 47.7 us; the launch traced here: 47.6 us
  Pallas kernels  45.7 us (96%)
  local copies, waits for them, and re-layouts  1.26 us (3%)
  between operations  0.64 us (1%)
    pallas_call x1, Pallas kernels, shards(): pl.pallas_call(functools.partial(kernel, sections, cands), out_shape=(jax...  45.7 us
    unnamed x2, local copies, waits for them, and re-layouts  1.26 us

profile of v6, /device:TPU:0, one launch (start us, length us, event | category | flops | bytes accessed | tf_op | source)
XLA Modules:
  0.0 47.6 jit_solution(6783470147894051349)
XLA Ops:
  0.6 45.7 %shard_map.59 = (f32[192,128]{1,0:T(8,128)S(1)}, f32[64,128]{1,0:T(8,128)S(1)}) custom-call(f32[32,192]{1,0:T(8,128)} %archive.1, f32[32,128]{1,0:T(8,128)} %candidates.1, f32[1,32]{1,0:T(1,128)} %bitcast.1, f32[192,1536]{1,0:T(8,128)} %factor.1), custom_call_target="tpu_custom_call" | custom-call | tf_op jit(solution)/shard_map/pallas_call | solution.py:478
  46.3 0.6 %copy.8 = f32[192,128]{1,0:T(8,128)} copy(f32[192,128]{1,0:T(8,128)S(1)} %get-tuple-element.4) | data formatting | bytes 196608
  47.0 0.6 %copy.9 = f32[64,128]{1,0:T(8,128)} copy(f32[64,128]{1,0:T(8,128)S(1)} %get-tuple-element.5) | data formatting | bytes 65536

commit v7 on v6

--- a/solution.py
+++ b/solution.py
@@ -163,6 +163,13 @@
     neighbours = cands + jnp.where(z > 0, 1, 0) + jnp.where(z < steps - 1, 1, 0)
     pl.semaphore_wait(barrier, neighbours)
 
+    def announce():
+        pl.semaphore_signal(ready, inc=1, device_id=(lax.rem(me + sections - 2, sections), c), device_id_type=MESH)
+
+    @pl.when(z == steps - 1)
+    def _():
+        announce()
+
     send_in = remote(archive, both_archive.at[y], in_send, in_recv, (partner, c))
     send_in.start()
 
@@ -254,14 +261,6 @@
         @pl.when(z > j)
         def _(j=j):
             turn_far(j)
-    @pl.when((z > 0) & (z < steps - 1))
-    def _():
-        pl.semaphore_wait(ready, 1)
-
-    @pl.when(z > 0)
-    def _():
-        pl.semaphore_signal(ready, inc=1, device_id=(lax.rem(me + sections - 2, sections), c), device_id_type=MESH)
-
     across_recv(0).wait_recv()
     upper_inverse = unpack(inverses[0], height)
     lower_inverse = unpack(inverses[1], height)
@@ -401,9 +400,13 @@
         def _():
             sums[z, group % ratio] = pieces[q]
 
-    @pl.when(z == 0)
+    @pl.when(z < steps - 1)
     def _():
         pl.semaphore_wait(ready, 1)
+
+    @pl.when((z > 0) & (z < steps - 1))
+    def _():
+        announce()
 
     piece(c)
     wait_peer(sibling)

time: 47.7 us -> 41.7 us (0.87)
  Pallas kernels: 45.7 us -> 39.6 us
    pallas_call x1, Pallas kernels: 45.7 us -> 39.6 us  [shards(): pl.pallas_call(functools.partial(kernel, sections, cands), out_shape=(jax...]
where the time goes in v7:
time: 41.7 us; the launch traced here: 41.5 us
  Pallas kernels  39.6 us (95%)
  local copies, waits for them, and re-layouts  1.26 us (3%)
  between operations  0.64 us (2%)
    pallas_call x1, Pallas kernels, shards(): pl.pallas_call(functools.partial(kernel, sections, cands), out_shape=(jax...  39.6 us
    unnamed x2, local copies, waits for them, and re-layouts  1.26 us

profile of v7, /device:TPU:0, one launch (start us, length us, event | category | flops | bytes accessed | tf_op | source)
XLA Modules:
  0.0 41.5 jit_solution(3925607056348441156)
XLA Ops:
  0.6 39.6 %shard_map.59 = (f32[192,128]{1,0:T(8,128)S(1)}, f32[64,128]{1,0:T(8,128)S(1)}) custom-call(f32[32,192]{1,0:T(8,128)} %archive.1, f32[32,128]{1,0:T(8,128)} %candidates.1, f32[1,32]{1,0:T(1,128)} %bitcast.1, f32[192,1536]{1,0:T(8,128)} %factor.1), custom_call_target="tpu_custom_call" | custom-call | tf_op jit(solution)/shard_map/pallas_call | solution.py:481
  40.3 0.6 %copy.8 = f32[192,128]{1,0:T(8,128)} copy(f32[192,128]{1,0:T(8,128)S(1)} %get-tuple-element.4) | data formatting | bytes 196608
  40.9 0.6 %copy.9 = f32[64,128]{1,0:T(8,128)} copy(f32[64,128]{1,0:T(8,128)S(1)} %get-tuple-element.5) | data formatting | bytes 65536

commit v8 on v7

--- a/solution.py
+++ b/solution.py
@@ -152,7 +152,7 @@
     block = jnp.where(y == 0, strip_of_pair[:, :height], strip_of_pair[:, height:])
     small = jnp.transpose(base_inverse(block))
     block = jnp.transpose(block)
-    small = grow_inverse(block, small, BASE, 2 * BASE)
+    small = grow_inverse(block, small, BASE, 4 * BASE)
     lengths_copy.wait()
     candidates_copy.wait()
     archive_copy.wait()
@@ -216,7 +216,7 @@
             chosen_copy(d).start()
         chosen[...] = own_candidates[...]
 
-    inverses[y] = pack(grow_inverse(block, small, 2 * BASE, height))
+    inverses[y] = pack(grow_inverse(block, small, 4 * BASE, height))
     across(0).start()
     for j in range(early, steps - 1):
         @pl.when(z > j)

time: 41.7 us -> 42.1 us (level)
  Pallas kernels: 39.6 us -> 40.1 us
    pallas_call x1, Pallas kernels: 39.6 us -> 40.1 us  [shards(): pl.pallas_call(functools.partial(kernel, sections, cands), out_shape=(jax...]
where the time goes in v8:
time: 42.1 us; the launch traced here: 42 us
  Pallas kernels  40.1 us (95%)
  local copies, waits for them, and re-layouts  1.26 us (3%)
  between operations  0.64 us (2%)
    pallas_call x1, Pallas kernels, shards(): pl.pallas_call(functools.partial(kernel, sections, cands), out_shape=(jax...  40.1 us
    unnamed x2, local copies, waits for them, and re-layouts  1.26 us

profile of v8, /device:TPU:0, one launch (start us, length us, event | category | flops | bytes accessed | tf_op | source)
XLA Modules:
  0.0 42.0 jit_solution(1591720437063470777)
XLA Ops:
  0.6 40.1 %shard_map.59 = (f32[192,128]{1,0:T(8,128)S(1)}, f32[64,128]{1,0:T(8,128)S(1)}) custom-call(f32[32,192]{1,0:T(8,128)} %archive.1, f32[32,128]{1,0:T(8,128)} %candidates.1, f32[1,32]{1,0:T(1,128)} %bitcast.1, f32[192,1536]{1,0:T(8,128)} %factor.1), custom_call_target="tpu_custom_call" | custom-call | tf_op jit(solution)/shard_map/pallas_call | solution.py:481
  40.7 0.6 %copy.8 = f32[192,128]{1,0:T(8,128)} copy(f32[192,128]{1,0:T(8,128)S(1)} %get-tuple-element.4) | data formatting | bytes 196608
  41.4 0.6 %copy.9 = f32[64,128]{1,0:T(8,128)} copy(f32[64,128]{1,0:T(8,128)S(1)} %get-tuple-element.5) | data formatting | bytes 65536
